TPU v7x, 32 devices: a whole 2x2x4 slice. The times are simulated.
32 devices in a mesh: row: 4 (over z), col: 8 (over y, x, core).
Axes of the slice: x: 2, y: 2, z: 4, core: 2. Of those that a mesh axis runs over, the one named last changes fastest.
Arguments:
- spectra: bfloat16 [256, 256, 512], P(('row', 'col')), may hold values from 0.05 to 20000
- sensor_ids: int32 [256, 1], P(('row', 'col')), may hold values from 0 to 31, as said below
- permutation: int32 [256], P(('row', 'col')), may hold values from 0 to 255, as said below
- w_enc1: bfloat16 [2048, 256], replicated, may hold values from -0.125 to 0.125
- w_enc2: bfloat16 [1024, 256], replicated, may hold values from -0.1875 to 0.1875
- w_dec1: bfloat16 [256, 1024], replicated, may hold values from -0.25 to 0.25
- w_dec2: bfloat16 [256, 2048], replicated, may hold values from -0.25 to 0.25
Outputs:
- grad_enc1: float32 [2048, 256], replicated
- grad_enc2: float32 [1024, 256], replicated
- grad_dec1: float32 [256, 1024], replicated
- grad_dec2: float32 [256, 2048], replicated
Inputs may be any that keep to these rules, and one draw needn't show every extreme that they name: `sensor_ids`: every sensor from 0 to 31 recorded exactly 8 windows. A permutation of all slots; the 8 windows of the ingest device with indices (a, b) go to 8 different trainers, one to each trainer whose col index c has c // 2 = a; each trainer thus receives one window from each ingest device of one row index.
All inputs are finite; a program needn't handle non-finite values.
Results may differ from a plain program's by a relative error of at most 0.004.
Values may be sent and summed in bfloat16 or wider, within the bound.
A program may use at most 192 MiB of HBM per device.

v0:
```python
import jax
import jax.numpy as jnp
from jax import lax
from jax.sharding import PartitionSpec as P

WIN_SENSOR = 8


EPS = 1e-05


def frame_taps(values):
    windows, length, channels = values.shape
    padded = jnp.pad(values, ((0, 0), (1, 1), (0, 0)))
    paired = padded.reshape(windows, length // 2 + 1, 2 * channels)
    return jnp.concatenate([paired[:, :-1], paired[:, 1:]], axis=2)


def fold_taps(stacked):
    windows, length, columns = stacked.shape
    channels = columns // 4
    pieces = stacked.reshape(windows, length, 4, channels)
    blank = jnp.zeros((windows, 1, channels), stacked.dtype)
    even_rows = pieces[:, :, 1] + jnp.concatenate([blank, pieces[:, :-1, 3]], axis=1)
    odd_rows = pieces[:, :, 2] + jnp.concatenate([pieces[:, 1:, 0], blank], axis=1)
    return jnp.stack([even_rows, odd_rows], axis=2).reshape(windows, 2 * length, channels)


def silu_slope(values):
    logistic = jax.nn.sigmoid(values)
    return logistic * (1.0 + values * (1.0 - logistic))


def forward_dot(values, weight):
    flat = values.reshape(-1, values.shape[-1])
    result = jnp.dot(flat, weight, preferred_element_type=jnp.float32)
    return result.reshape(values.shape[:-1] + (weight.shape[1],))


def backward_dot(values, weight):
    flat = values.reshape(-1, values.shape[-1])
    result = lax.dot_general(
        flat, weight, (((1,), (1,)), ((), ())), preferred_element_type=jnp.float32
    )
    return result.reshape(values.shape[:-1] + (weight.shape[0],))


def sensor_table(sensor_col, sensor_total):
    return (sensor_col[:, None] == jnp.arange(sensor_total, dtype=jnp.int32)[None, :]).astype(
        jnp.float32
    )


def standardize(log_power, table, center, factor):
    shift = jnp.dot(table, center, precision=lax.Precision.HIGHEST)
    stretch = jnp.dot(table, factor, precision=lax.Precision.HIGHEST)
    return ((log_power - shift[:, None, :]) * stretch[:, None, :]).astype(jnp.bfloat16)


def layer_sum(left, right):
    left_flat = left.reshape(-1, left.shape[-1])
    right_flat = right.reshape(-1, right.shape[-1])
    gradient = jnp.einsum("rk,ro->ko", left_flat, right_flat, preferred_element_type=jnp.float32)
    return gradient


def local(spectra, sensor_ids, permutation, w_enc1, w_enc2, w_dec1, w_dec2):
    window_count = spectra.shape[0]
    frame_count = spectra.shape[1]
    row_count = lax.axis_size("row")
    col_count = lax.axis_size("col")
    total_windows = window_count * row_count * col_count
    sensor_total = total_windows // WIN_SENSOR
    sensor_col = sensor_ids[:, 0]
    table = sensor_table(sensor_col, sensor_total)
    log_power = jnp.log1p(spectra.astype(jnp.float32))
    win_sums = jnp.sum(log_power, axis=1)
    win_squares = jnp.sum(log_power * log_power, axis=1)
    totals = jnp.einsum("ws,wb->sb", table, win_sums, precision=lax.Precision.HIGHEST)
    squares = jnp.einsum("ws,wb->sb", table, win_squares, precision=lax.Precision.HIGHEST)
    counts = jnp.sum(table, axis=0) * frame_count
    totals, squares, counts = lax.psum((totals, squares, counts), ("row", "col"))
    center = totals / counts[:, None]
    factor = lax.rsqrt(squares / counts[:, None] - center * center + EPS)
    payload = standardize(log_power, table, center, factor)
    labels = jnp.stack([permutation, sensor_col], axis=1)
    positions = jnp.arange(window_count, dtype=jnp.int32)
    ranking = jnp.argsort(labels[:, 0] // col_count // col_count * col_count + positions)
    payload, labels = (
        lax.all_to_all(payload[ranking], "row", split_axis=0, concat_axis=0, tiled=True),
        lax.all_to_all(labels[ranking], "row", split_axis=0, concat_axis=0, tiled=True),
    )
    ranking = jnp.argsort(labels[:, 0] // col_count % col_count)
    payload, labels = (
        lax.all_to_all(payload[ranking], "col", split_axis=0, concat_axis=0, tiled=True),
        lax.all_to_all(labels[ranking], "col", split_axis=0, concat_axis=0, tiled=True),
    )
    stem_taps = frame_taps(payload)
    enc1_pre = forward_dot(stem_taps, w_enc1)
    middle = jnp.mean(enc1_pre, axis=(0, 1))
    variance = jnp.mean(jnp.square(enc1_pre - middle), axis=(0, 1))
    inverse = lax.rsqrt(variance + EPS)
    enc1_hat = (enc1_pre - middle) * inverse
    enc1_out = jax.nn.silu(enc1_hat).astype(jnp.bfloat16)
    mid_taps = frame_taps(enc1_out)
    enc2_pre = forward_dot(mid_taps, w_enc2)
    enc2_out = jax.nn.silu(enc2_pre).astype(jnp.bfloat16)
    dec1_pre = fold_taps(forward_dot(enc2_out, w_dec1))
    dec1_out = jax.nn.silu(dec1_pre).astype(jnp.bfloat16)
    rebuilt = fold_taps(forward_dot(dec1_out, w_dec2))
    delta_out = ((rebuilt - payload.astype(jnp.float32)) / total_windows).astype(jnp.bfloat16)
    out_taps = frame_taps(delta_out)
    grad_dec2 = layer_sum(dec1_out, out_taps)
    delta_dec1 = (backward_dot(out_taps, w_dec2) * silu_slope(dec1_pre)).astype(jnp.bfloat16)
    dec_taps = frame_taps(delta_dec1)
    grad_dec1 = layer_sum(enc2_out, dec_taps)
    delta_enc2 = (backward_dot(dec_taps, w_dec1) * silu_slope(enc2_pre)).astype(jnp.bfloat16)
    grad_enc2 = layer_sum(mid_taps, delta_enc2)
    back_enc1 = fold_taps(backward_dot(delta_enc2, w_enc2)) * silu_slope(enc1_hat)
    first_mean = jnp.mean(back_enc1, axis=(0, 1))
    second_mean = jnp.mean(back_enc1 * enc1_hat, axis=(0, 1))
    delta_enc1 = ((back_enc1 - first_mean - enc1_hat * second_mean) * inverse).astype(jnp.bfloat16)
    grad_enc1 = layer_sum(stem_taps, delta_enc1)
    grad_enc1, grad_enc2, grad_dec1, grad_dec2 = lax.psum(
        (grad_enc1, grad_enc2, grad_dec1, grad_dec2), ("row", "col")
    )
    return (grad_enc1, grad_enc2, grad_dec1, grad_dec2)


def solution(mesh):
    return jax.shard_map(
        local,
        mesh=mesh,
        in_specs=(
            P(("row", "col"), None, None),
            P(("row", "col"), None),
            P(("row", "col")),
            P(),
            P(),
            P(),
            P(),
        ),
        out_specs=(P(), P(), P(), P()),
        check_vma=False,
    )
```

profile of v0, /device:TPU:0, one launch (start us, length us, event | category | flops | bytes accessed | tf_op | source)
XLA Modules:
  0.0 448.1 jit_solution(4792768739675535872)
XLA Ops:
  7.3 3.6 fusion.2
  15.1 6.3 %all-to-all-start.1 = ((s32[4,2,2]{1,2,0:T(2,128)}), s32[4,2,2]{1,2,0:T(2,128)S(1)}, u32[]{:S(2)}, u32[]{:S(2)}) async-start(s32[4,2,2]{1,2,0:T(2,128)} %copy.131), calls=%async_computation.1 | async-start | bytes 8192 | tf_op jit(solution)/shard_map/all_to_all | solution.py:91
  21.4 40.8 %psum.50 = f32[32]{0:T(128)S(1)} all-reduce(f32[32]{0:T(128)S(1)} %broadcast_multiply_fusion.3), channel_id=1, replica_groups=mesh['row'=4,'col'=8] {'row','col'}, use_global_device_ids=true, to_apply=%region_3.0 | all-reduce | flops 32 | bytes 256 | tf_op jit(solution)/shard_map/psum | solution.py:82
  62.2 77.7 %all-reduce.17.cloned.1.call-done = (f32[32,512]{1,0:T(8,128)}, f32[32,512]{1,0:T(8,128)}) async-done(((f32[32,512]{1,0:T(8,128)}, f32[32,512]{1,0:T(8,128)}), (f32[32,512]{1,0:T(8,128)}, f32[32,512]{1,0:T(8,128)})) %all-reduce.17.cloned.1.call-update) | async-done | bytes 131088 | tf_op jit(solution)/shard_map/psum | solution.py:82
  142.1 3.0 multiply_convert_fusion
  145.1 3.6 gather_fusion
  148.7 3.6 all-to-all-start
  153.4 46.6 %all-to-all-done = bf16[8,256,512]{2,1,0:T(8,128)(2,1)S(1)} async-done(((bf16[8,256,512]{2,1,0:T(8,128)(2,1)}), bf16[8,256,512]{2,1,0:T(8,128)(2,1)S(1)}, u32[]{:S(2)}, u32[]{:S(2)}) %all-to-all-start) | async-done | bytes 2097184 | tf_op jit(solution)/shard_map/all_to_all | solution.py:90
  200.0 2.0 gather_fusion.2
  202.0 3.6 all-to-all-start.2
  205.7 2.0 copy.171
  207.7 2.4 copy.174
  210.1 22.1 %all-to-all-done.2 = bf16[8,256,512]{2,1,0:T(8,128)(2,1)S(1)} async-done(((bf16[8,256,512]{2,1,0:T(8,128)(2,1)}), bf16[8,256,512]{2,1,0:T(8,128)(2,1)S(1)}, u32[]{:S(2)}, u32[]{:S(2)}) %all-to-all-start.2) | async-done | bytes 2097184 | tf_op jit(solution)/shard_map/all_to_all | solution.py:95
  242.9 1.8 copy.154
  244.7 3.0 reshape.96
  252.9 2.4 copy.149
  255.3 2.7 fusion.1
  262.7 1.5 fusion.7
  264.1 2.9 convolution_bitcast_fusion
  269.0 1.5 convolution_bitcast_fusion.2
  270.5 1.4 convolution_bitcast_fusion.3
  274.9 5.1 %convolution_bitcast_fusion.1 = f32[2048,256]{1,0:T(8,128)} fusion(bf16[8,128,2048]{2,1,0:T(8,128)(2,1)} %copy-done.14, f32[8,128,256]{2,1,0:T(8,128)S(1)} %copy-done.3, f32[256]{0:T(256)S(1)} %get-tuple-element.42, f32[256]{0:T(256)S(1)} %get-tuple-element.43, f32[256]{0:T(256)S(1)} %add_rsqrt_fusion, f32[256]{0:T(256)S(1)} %broadcast_multiply_fusion.2, ...), kind=kOutput, calls=%fused_computation.12 | convolution fusion | flops 1077673984 | bytes 8392704 | tf_op jit(solution)/shard_map/rk,ro->ko/dot_general | solution.py:63
  280.0 154.3 %all-reduce.15.cloned.1.call-done = (f32[2048,256]{1,0:T(8,128)}, f32[1024,256]{1,0:T(8,128)}, f32[256,1024]{1,0:T(8,128)}, f32[256,2048]{1,0:T(8,128)}) async-done(((f32[2048,256]{1,0:T(8,128)}, f32[1024,256]{1,0:T(8,128)}, f32[256,1024]{1,0:T(8,128)}, f32[256,2048]{1,0:T(8,128)}), (f32[2048,256]{1,0:T(8,128)}, f32[1024,256]{1,0:T(8,128)}, f32[256,1024]{1,0:T(8,128)}, ...) | async-done | bytes 6291472 | tf_op jit(solution)/shard_map/psum | solution.py:124
  434.3 3.2 copy.221
  (118 shorter events, 36.1 us)
Async XLA Ops:
  7.2 229.2 %copy-start = (bf16[2048,256]{1,0:T(8,128)(2,1)S(1)}, bf16[2048,256]{1,0:T(8,128)(2,1)}, u32[]{:S(2)}) copy-start(bf16[2048,256]{1,0:T(8,128)(2,1)} %param.10) | copy-start | bytes 3145732
  7.2 134.9 %copy-start.4 = (bf16[8,256,512]{2,1,0:T(8,128)(2,1)S(1)}, bf16[8,256,512]{2,1,0:T(8,128)(2,1)}, u32[]{:S(2)}) copy-start(bf16[8,256,512]{2,1,0:T(8,128)(2,1)} %param.7) | copy-start | bytes 6291460
  7.2 3.6 copy-start.20
  7.2 5.6 %copy-start.21 = (s32[8]{0:T(128)S(1)}, s32[8]{0:T(128)}, u32[]{:S(2)}) copy-start(s32[8]{0:T(128)} %param.9) | copy-start | bytes 100
  7.2 132.7 %all-reduce.17.cloned.1.call-start = ((), (), s32[]{:S(2)}) async-start(), calls=%async_computation.4 | async-start | bytes 262144 | tf_op jit(solution)/shard_map/psum | solution.py:82
  15.1 133.6 %all-to-all-start.1 = ((s32[4,2,2]{1,2,0:T(2,128)}), s32[4,2,2]{1,2,0:T(2,128)S(1)}, u32[]{:S(2)}, u32[]{:S(2)}) async-start(s32[4,2,2]{1,2,0:T(2,128)} %copy.131), calls=%async_computation.1 | async-start | bytes 8192 | tf_op jit(solution)/shard_map/all_to_all | solution.py:91
  148.7 51.3 %all-to-all-start = ((bf16[8,256,512]{2,1,0:T(8,128)(2,1)}), bf16[8,256,512]{2,1,0:T(8,128)(2,1)S(1)}, u32[]{:S(2)}, u32[]{:S(2)}) async-start(bf16[8,256,512]{2,1,0:T(8,128)(2,1)} %gather_fusion), calls=%async_computation | async-start | bytes 4194304 | tf_op jit(solution)/shard_map/all_to_all | solution.py:90
  202.0 30.2 %all-to-all-start.2 = ((bf16[8,256,512]{2,1,0:T(8,128)(2,1)}), bf16[8,256,512]{2,1,0:T(8,128)(2,1)S(1)}, u32[]{:S(2)}, u32[]{:S(2)}) async-start(bf16[8,256,512]{2,1,0:T(8,128)(2,1)} %gather_fusion.2), calls=%async_computation.2 | async-start | bytes 4194304 | tf_op jit(solution)/shard_map/all_to_all | solution.py:95
  205.6 228.7 %all-reduce.15.cloned.1.call-start = ((), (), s32[]{:S(2)}) async-start(), calls=%async_computation.3 | async-start | bytes 12582912 | tf_op jit(solution)/shard_map/psum | solution.py:124
  236.4 1.9 copy-start.14
  239.3 1.0 copy-start.10
  239.4 1.4 copy-start.9
  244.7 4.3 copy-start.5
  261.1 1.2 copy-start.15
  261.1 1.5 copy-start.16
  267.3 1.0 copy-start.13
  267.3 1.2 copy-start.19
  269.0 1.5 copy-start.7
  270.5 1.4 copy-start.11
  272.8 1.6 copy-start.3
  434.3 3.2 copy-start.18
  434.3 4.2 copy-start.17
  437.5 2.0 copy-start.8
  438.5 2.4 copy-start.1
  (3 other events, 2.8 us)
Sparse Core Ops, SparseCore 0:
  14.3 125.5 all-reduce.16
  280.1 154.1 all-reduce.14
where the time goes:
time: 454 us; the launch traced here: 448 us
  waiting for transfers between devices  301 us (66%)
  local copies, waits for them, and re-layouts  41.5 us (9%)
  blocking collectives  40.8 us (9%)
  matrix products  20.7 us (5%)
  other arithmetic  15.8 us (3%)
  between operations  15 us (3%)
  starting transfers between devices  13.6 us (3%)
    psum x1, waiting for transfers between devices, local(): lax.psum((grad_enc1, grad_enc2, grad_dec1, grad_dec2), ('row', 'col'))  154 us
    psum x1, waiting for transfers between devices, local(): lax.psum((totals, squares, counts), ('row', 'col'))  77.7 us
    all_to_all x1, waiting for transfers between devices, local(): lax.all_to_all(payload[ranking], 'row', split_axis=0, concat_axis=0, tile...  46.6 us
    psum x1, blocking collectives, local(): lax.psum((totals, squares, counts), ('row', 'col'))  40.8 us
    all_to_all x1, waiting for transfers between devices, local(): lax.all_to_all(payload[ranking], 'col', split_axis=0, concat_axis=0, tile...  22.1 us
    unnamed x56, local copies, waits for them, and re-layouts  14.8 us
    dot_general x4, matrix products, layer_sum(): jnp.einsum('rk,ro->ko', left_flat, right_flat, preferred_element_type=jnp...  10.9 us
  transfers between devices with their start and end apart: 5, of which 4 were waited for; matrix products, arithmetic and copies ran while one was open for 4% of the time, Pallas kernels for 0%

commit v1 on v0

--- a/solution.py
+++ b/solution.py
@@ -71,29 +71,25 @@
     col_count = lax.axis_size("col")
     total_windows = window_count * row_count * col_count
     sensor_total = total_windows // WIN_SENSOR
+    per_row = col_count // row_count
     sensor_col = sensor_ids[:, 0]
+    trainer = permutation // window_count
+    target = trainer // col_count * per_row + trainer % per_row
+    ranking = jnp.argsort(target)
+    raw = lax.all_to_all(spectra[ranking], "col", split_axis=0, concat_axis=0, tiled=True)
+    labels = lax.all_to_all(sensor_col[ranking], "col", split_axis=0, concat_axis=0, tiled=True)
     table = sensor_table(sensor_col, sensor_total)
     log_power = jnp.log1p(spectra.astype(jnp.float32))
     win_sums = jnp.sum(log_power, axis=1)
     win_squares = jnp.sum(log_power * log_power, axis=1)
     totals = jnp.einsum("ws,wb->sb", table, win_sums, precision=lax.Precision.HIGHEST)
     squares = jnp.einsum("ws,wb->sb", table, win_squares, precision=lax.Precision.HIGHEST)
-    counts = jnp.sum(table, axis=0) * frame_count
-    totals, squares, counts = lax.psum((totals, squares, counts), ("row", "col"))
-    center = totals / counts[:, None]
-    factor = lax.rsqrt(squares / counts[:, None] - center * center + EPS)
-    payload = standardize(log_power, table, center, factor)
-    labels = jnp.stack([permutation, sensor_col], axis=1)
-    positions = jnp.arange(window_count, dtype=jnp.int32)
-    ranking = jnp.argsort(labels[:, 0] // col_count // col_count * col_count + positions)
-    payload, labels = (
-        lax.all_to_all(payload[ranking], "row", split_axis=0, concat_axis=0, tiled=True),
-        lax.all_to_all(labels[ranking], "row", split_axis=0, concat_axis=0, tiled=True),
-    )
-    ranking = jnp.argsort(labels[:, 0] // col_count % col_count)
-    payload, labels = (
-        lax.all_to_all(payload[ranking], "col", split_axis=0, concat_axis=0, tiled=True),
-        lax.all_to_all(labels[ranking], "col", split_axis=0, concat_axis=0, tiled=True),
+    totals, squares = lax.psum((totals, squares), ("row", "col"))
+    count = WIN_SENSOR * frame_count
+    center = totals / count
+    factor = lax.rsqrt(squares / count - center * center + EPS)
+    payload = standardize(
+        jnp.log1p(raw.astype(jnp.float32)), sensor_table(labels, sensor_total), center, factor
     )
     stem_taps = frame_taps(payload)
     enc1_pre = forward_dot(stem_taps, w_enc1)
@@ -121,10 +117,11 @@
     second_mean = jnp.mean(back_enc1 * enc1_hat, axis=(0, 1))
     delta_enc1 = ((back_enc1 - first_mean - enc1_hat * second_mean) * inverse).astype(jnp.bfloat16)
     grad_enc1 = layer_sum(stem_taps, delta_enc1)
-    grad_enc1, grad_enc2, grad_dec1, grad_dec2 = lax.psum(
-        (grad_enc1, grad_enc2, grad_dec1, grad_dec2), ("row", "col")
+    grads = tuple(
+        value.astype(jnp.bfloat16) for value in (grad_enc1, grad_enc2, grad_dec1, grad_dec2)
     )
-    return (grad_enc1, grad_enc2, grad_dec1, grad_dec2)
+    grads = lax.psum(grads, ("row", "col"))
+    return tuple(value.astype(jnp.float32) for value in grads)
 
 
 def solution(mesh):

time: 454 us -> 366 us (0.81)
  blocking collectives: 40.8 us -> 0 us
  waiting for transfers between devices: 301 us -> 264 us
  local copies, waits for them, and re-layouts: 41.5 us -> 33.8 us
  other arithmetic: 15.8 us -> 21.4 us
  starting transfers between devices: 13.6 us -> 8.86 us
    all_to_all x3 -> x2, waiting for transfers between devices: 68.7 us -> 1 us  [the longest x1 1 us: local(): lax.all_to_all(sensor_col[ranking], 'col', split_axis=0, concat_axis=0, t...]
    psum x1 -> x0, blocking collectives: 40.8 us -> none  [local(): lax.psum((totals, squares, counts), ('row', 'col'))]
    psum x2, waiting for transfers between devices: 232 us -> 263 us  [the longest x1 138 us: local(): grads = lax.psum(grads, ('row', 'col'))]
    convert_element_type x0 -> x4, other arithmetic: none -> 6.48 us  [local(): return tuple((value.astype(jnp.float32) for value in grads))]
    unnamed x56 -> x48, local copies, waits for them, and re-layouts: 14.8 us -> 8.61 us
    all_to_all x3 -> x2, starting transfers between devices: 13.5 us -> 8.78 us  [the longest x1 5.17 us: local(): lax.all_to_all(sensor_col[ranking], 'col', split_axis=0, concat_axis=0, t...]
  transfers between devices with their start and end apart: 5 -> 4, of which waited for: 4 -> 3; matrix products, arithmetic and copies ran while one was open for 4% -> 4% of each run, Pallas kernels for 0% -> 0%
where the time goes in v1:
time: 366 us; the launch traced here: 363 us
  waiting for transfers between devices  264 us (72%)
  local copies, waits for them, and re-layouts  33.8 us (9%)
  other arithmetic  21.4 us (6%)
  matrix products  19.7 us (5%)
  between operations  14.9 us (4%)
  starting transfers between devices  8.86 us (2%)
    psum x1, waiting for transfers between devices, local(): grads = lax.psum(grads, ('row', 'col'))  138 us
    psum x1, waiting for transfers between devices, local(): totals, squares = lax.psum((totals, squares), ('row', 'col'))  125 us
    dot_general x4, matrix products, layer_sum(): jnp.einsum('rk,ro->ko', left_flat, right_flat, preferred_element_type=jnp...  9.62 us
    unnamed x48, local copies, waits for them, and re-layouts  8.61 us
  transfers between devices with their start and end apart: 4, of which 3 were waited for; matrix products, arithmetic and copies ran while one was open for 4% of the time, Pallas kernels for 0%

profile of v1, /device:TPU:0, one launch (start us, length us, event | category | flops | bytes accessed | tf_op | source)
XLA Modules:
  0.0 362.7 jit_solution(9112741456849592820)
XLA Ops:
  8.9 1.3 gather_fusion.1
  10.9 5.2 %all-to-all-start.1 = ((s32[8,1,1]{2,1,0:T(1,128)}), s32[8,1,1]{2,1,0:T(1,128)S(1)}, u32[]{:S(2)}, u32[]{:S(2)}) async-start(s32[8,1,1]{2,1,0:T(1,128)} %copy.117), calls=%async_computation.1 | async-start | bytes 8192 | tf_op jit(solution)/shard_map/all_to_all | solution.py:80
  16.1 3.6 gather_fusion
  20.7 3.6 all-to-all-start
  24.3 3.4 fusion.2
  29.7 2.0 copy.154
  31.7 2.4 copy.157
  34.4 124.9 %all-reduce.15.cloned.1.call-done = (f32[32,512]{1,0:T(8,128)}, f32[32,512]{1,0:T(8,128)}) async-done(((f32[32,512]{1,0:T(8,128)}, f32[32,512]{1,0:T(8,128)}), (f32[32,512]{1,0:T(8,128)}, f32[32,512]{1,0:T(8,128)})) %all-reduce.15.cloned.1.call-update) | async-done | bytes 131088 | tf_op jit(solution)/shard_map/psum | solution.py:87
  161.4 1.7 multiply_convert_fusion
  173.9 1.8 copy.139
  175.6 3.0 reshape.97
  178.6 1.3 copy.128
  180.0 1.5 fusion.25
  183.9 2.4 copy.134
  186.3 3.7 %fusion.1 = bf16[8,256,512]{2,1,0:T(8,128)(2,1)S(1)} fusion(f32[8,256,512]{2,0,1:T(8,128)S(1)} %bitcast.158, f32[8,512]{1,0:T(8,128)S(1)} %fusion.38, f32[8,512]{1,0:T(8,128)S(1)} %fusion.45, bf16[8,256,512]{2,1,0:T(8,128)(2,1)S(1)} %all-to-all-done), kind=kLoop, calls=%fused_computation.5 | loop fusion | flops 8388608 | bytes 8421376 | tf_op jit(solution)/shard_map/convert_element_type | solution.py:107
  191.9 1.4 copy_dynamic-update-slice_fusion.1
  194.9 1.4 fusion.9
  196.3 2.3 fusion.4
  200.6 1.3 fusion.11
  201.9 1.3 fusion.10
  206.1 4.8 %fusion.3 = bf16[2048,256]{1,0:T(8,128)(2,1)} fusion(bf16[8,128,2048]{2,1,0:T(8,128)(2,1)} %copy-done.14, f32[8,128,256]{2,1,0:T(8,128)S(1)} %copy-done.4, f32[256]{0:T(256)S(1)} %get-tuple-element.40, f32[256]{0:T(256)S(1)} %get-tuple-element.41, f32[256]{0:T(256)S(1)} %add_rsqrt_fusion, f32[256]{0:T(256)S(1)} %broadcast_multiply_fusion.2, ...), kind=kOutput, calls=%fused_computation.12 | convolution fusion | flops 1078198272 | bytes 7344128 | tf_op jit(solution)/shard_map/rk,ro->ko/dot_general | solution.py:63
  210.9 138.0 %all-reduce.17.cloned.1.call-done = (bf16[2048,256]{1,0:T(8,128)(2,1)}, bf16[1024,256]{1,0:T(8,128)(2,1)}, bf16[256,1024]{1,0:T(8,128)(2,1)}, bf16[256,2048]{1,0:T(8,128)(2,1)}) async-done(((bf16[2048,256]{1,0:T(8,128)(2,1)}, bf16[1024,256]{1,0:T(8,128)(2,1)}, bf16[256,1024]{1,0:T(8,128)(2,1)}, bf16[256,2048]{1,0:T(8,128)(2,1)}), (bf16[2048,256]{1,0:T(8,128)(2,1)}, bf16[1024,256]{1,0:T(8,128)(2,1)}, ...) | async-done | bytes 3145744 | tf_op jit(solution)/shard_map/psum | solution.py:123
  348.9 2.8 convert_element_type.91
  353.8 1.6 convert_element_type.98
  (100 shorter events, 31.0 us)
Async XLA Ops:
  7.2 160.1 %copy-start = (bf16[2048,256]{1,0:T(8,128)(2,1)S(1)}, bf16[2048,256]{1,0:T(8,128)(2,1)}, u32[]{:S(2)}) copy-start(bf16[2048,256]{1,0:T(8,128)(2,1)} %param.10) | copy-start | bytes 3145732
  10.9 9.8 %all-to-all-start.1 = ((s32[8,1,1]{2,1,0:T(1,128)}), s32[8,1,1]{2,1,0:T(1,128)S(1)}, u32[]{:S(2)}, u32[]{:S(2)}) async-start(s32[8,1,1]{2,1,0:T(1,128)} %copy.117), calls=%async_computation.1 | async-start | bytes 8192 | tf_op jit(solution)/shard_map/all_to_all | solution.py:80
  20.7 140.7 %all-to-all-start = ((bf16[8,256,512]{2,1,0:T(8,128)(2,1)}), bf16[8,256,512]{2,1,0:T(8,128)(2,1)S(1)}, u32[]{:S(2)}, u32[]{:S(2)}) async-start(bf16[8,256,512]{2,1,0:T(8,128)(2,1)} %gather_fusion), calls=%async_computation | async-start | bytes 4194304 | tf_op jit(solution)/shard_map/all_to_all | solution.py:79
  24.3 3.5 copy-start.2
  24.3 135.0 %all-reduce.15.cloned.1.call-start = ((), (), s32[]{:S(2)}) async-start(), calls=%async_computation.2 | async-start | bytes 262144 | tf_op jit(solution)/shard_map/psum | solution.py:87
  29.6 319.3 %all-reduce.17.cloned.1.call-start = ((), (), s32[]{:S(2)}) async-start(), calls=%async_computation.3 | async-start | bytes 6291456 | tf_op jit(solution)/shard_map/psum | solution.py:123
  167.3 1.9 copy-start.14
  169.3 1.0 copy-start.3
  170.2 1.0 copy-start.9
  170.3 1.4 copy-start.8
  171.3 1.0 copy-start.6
  171.7 0.8 copy-start.11
  175.6 4.3 %copy-start.5 = (bf16[2048,256]{1,0:T(8,128)(2,1)S(1)}, bf16[2048,256]{1,0:T(8,128)(2,1)}, u32[]{:S(2)}) copy-start(bf16[2048,256]{1,0:T(8,128)(2,1)} %copy.157) | copy-start | bytes 3145732
  193.3 1.2 copy-start.15
  193.3 1.5 copy-start.16
  198.9 1.0 copy-start.12
  198.9 1.2 copy-start.19
  200.6 1.3 copy-start.7
  201.9 1.3 copy-start.10
  204.0 1.6 copy-start.4
  348.9 2.8 copy-start.18
  348.9 3.8 %copy-start.17 = (bf16[256,1024]{1,0:T(8,128)(2,1)S(1)}, bf16[256,1024]{1,0:T(8,128)(2,1)}, u32[]{:S(2)}) copy-start(bf16[256,1024]{1,0:T(8,128)(2,1)} %get-tuple-element.14) | copy-start | bytes 1572868
  351.7 2.1 copy-start.13
  352.7 2.7 copy-start.1
Sparse Core Ops, SparseCore 0:
  31.4 127.8 all-reduce.14
  211.0 137.8 all-reduce.16
